TPU v7x, 128 devices: a whole 4x4x4 slice. The times are simulated.
128 devices in a mesh: front: 16 (over x, z), grp: 8 (over y, core).
Axes of the slice: x: 4, y: 4, z: 4, core: 2. Of those that a mesh axis runs over, the one named last changes fastest.
Arguments:
- front_block: float32 [16, 16384, 1408], P('front', 'grp'), as said below
- child_blocks: float32 [16, 8, 4, 16, 1408], P('front', 'grp'), may hold values from -0.5 to 0.5
- child_rows: int32 [16, 8, 4, 16], P('front', 'grp'), may hold values from 0 to 2047
- child_dest: int32 [16, 8, 4, 1], P('front', 'grp'), may hold values from 0 to 15; in each aligned block of 4 rows (0 to 3, 4 to 7, ..., all dimensions but the last counted through in order) at most 2 rows name the same one
- panel_owner: int32 [16], P('front'), may hold values from 0 to 7
Outputs:
- panel_factor: float32 [16, 16384, 512], P('front', 'grp')
- schur_block: float32 [16, 16384, 896], P('front', 'grp')
Inputs may be any that keep to these rules, and one draw needn't show every extreme that they name: `child_dest`: among the 4 blocks of one device no front is named more than 2 times, and in every draw some device names some front exactly 2 times. `front_block`: for every front and row block, the first 512 rows' leading 512 x 512 block has a positive diagonal that dominates; other entries lie within -2.3 to 2.3.
All inputs are finite; a program needn't handle non-finite values.
Results may differ from a plain program's by a relative error of at most 0.0003.
Values sent between devices are 32-bit elements; how exact they have to be, the bound alone decides.
A program may use at most 128 MiB of HBM per device.

v0:
```python
import jax
import jax.numpy as jnp
from jax import lax
from jax.sharding import PartitionSpec as P

PB = 512
CAP = 2


def spread(array, axis, root):
    mine = lax.axis_index(axis) == root
    return lax.psum(jnp.where(mine, array, jnp.zeros_like(array)), axis)


def right_solve(factor, rows):
    return lax.linalg.triangular_solve(factor, rows, left_side=False, lower=True, transpose_a=True)


def pack_slots(values, slot_index, front_count):
    empty = jnp.zeros((front_count * CAP,) + values.shape[1:], values.dtype)
    filled = empty.at[slot_index].set(values)
    return filled.reshape((front_count, CAP) + values.shape[1:])


def local(front_block, child_blocks, child_rows, child_dest, panel_owner):
    local_rows = front_block[0]
    front_count = lax.axis_size("front")
    blocks = child_blocks[0, 0]
    row_lists = child_rows[0, 0]
    target_front = child_dest[0, 0, :, 0]
    block_count = target_front.shape[0]
    position = jnp.arange(block_count, dtype=jnp.int32)
    same_front = target_front[:, None] == target_front[None, :]
    earlier = position[None, :] < position[:, None]
    slot_index = target_front * CAP + jnp.sum((same_front & earlier).astype(jnp.int32), axis=1)
    send_rows = pack_slots(row_lists, slot_index, front_count)
    panel_cols = PB
    send_blocks = pack_slots(blocks, slot_index, front_count)
    got_blocks, got_rows = (
        lax.all_to_all(send_blocks, "front", split_axis=0, concat_axis=0, tiled=True),
        lax.all_to_all(send_rows, "front", split_axis=0, concat_axis=0, tiled=True),
    )
    flat_rows = got_rows.reshape(-1)
    local_rows = local_rows.at[flat_rows].add(got_blocks.reshape(-1, local_rows.shape[1]))
    win_cols = local_rows.shape[1] - panel_cols
    owner_index = panel_owner[0]
    is_owner = lax.axis_index("grp") == owner_index
    pivot_block = spread(local_rows[:panel_cols, :panel_cols], "grp", owner_index)
    symmetric = 0.5 * (pivot_block + pivot_block.T)
    pivot_factor = jnp.linalg.cholesky(symmetric)
    solved = right_solve(pivot_factor, local_rows[:, :panel_cols])
    window = spread(solved[panel_cols : panel_cols + win_cols], "grp", owner_index)
    schur_part = local_rows[:, panel_cols:] - jnp.dot(
        solved, window.T, precision=lax.Precision.HIGHEST
    )
    top_rows = jnp.where(is_owner, pivot_factor, solved[:panel_cols])
    panel_rows = jnp.concatenate([top_rows, solved[panel_cols:]], axis=0)
    return (panel_rows[None], schur_part[None])


def solution(mesh):
    placed = (
        P("front", "grp", None),
        P("front", "grp", None, None, None),
        P("front", "grp", None, None),
        P("front", "grp", None, None),
        P("front"),
    )
    return jax.shard_map(
        local,
        mesh=mesh,
        in_specs=placed,
        out_specs=(P("front", "grp", None), P("front", "grp", None)),
        check_vma=False,
    )
```

profile of v0, /device:TPU:0, one launch (start us, length us, event | category | flops | bytes accessed | tf_op | source)
XLA Modules:
  0.0 405.6 jit_solution(12922909138778709445)
XLA Ops:
  7.2 9.4 %copy.71 = f32[1,2048,1408]{2,1,0:T(8,128)} copy(f32[1,2048,1408]{2,1,0:T(8,128)} %param.5) | data formatting | bytes 23068672
  16.8 1.2 scatter_custom_fusion
  18.0 8.0 %all-to-all-start = ((s32[16,2,16]{2,1,0:T(2,128)}), s32[16,2,16]{2,1,0:T(2,128)S(1)}, u32[]{:S(2)}, u32[]{:S(2)}) async-start(s32[16,2,16]{2,1,0:T(2,128)} %bitcast.7), calls=%async_computation | async-start | bytes 32768 | tf_op jit(solution)/shard_map/all_to_all | solution.py:41
  26.0 1.8 broadcast_in_dim.26
  27.7 2.3 scatter_fusion
  30.1 3.5 all-to-all-done
  33.6 3.7 all-to-all-start.1
  38.1 38.4 %all-to-all-done.1 = f32[16,2,16,1408]{3,2,1,0:T(8,128)S(1)} async-done(((f32[16,2,16,1408]{3,2,1,0:T(8,128)}), f32[16,2,16,1408]{3,2,1,0:T(8,128)S(1)}, u32[]{:S(2)}, u32[]{:S(2)}) %all-to-all-start.1) | async-done | bytes 2883616 | tf_op jit(solution)/shard_map/all_to_all | solution.py:40
  76.6 14.0 %scatter_fusion.1 = f32[2048,1408]{1,0:T(8,128)} fusion(f32[2048,1408]{1,0:T(8,128)} %bitcast.75, s32[512]{0:T(512)S(1)} %bitcast.78, f32[512,1408]{1,0:T(8,128)S(1)} %bitcast.76), kind=kCustom, calls=%fused_computation.2 | custom fusion | flops 720896 | bytes 8652800 | tf_op jit(solution)/shard_map/scatter-add | solution.py:44
  90.6 1.3 slice.139
  91.9 0.3 copy.48
  92.2 1.1 broadcast_select_fusion
  93.6 60.5 %all-reduce.4.cloned.1.call-done = f32[512,512]{0,1:T(8,128)} async-done(((f32[512,512]{0,1:T(8,128)}), f32[512,512]{0,1:T(8,128)}) %all-reduce.4.cloned.1.call-update) | async-done | bytes 1048592 | tf_op jit(solution)/shard_map/psum | solution.py:12
  154.1 1.6 copy.34
  155.6 1.5 fusion.16
  157.1 0.3 copy.35
  157.5 0.2 fusion.15
  157.7 11.7 %cholesky.103 = f32[128,128]{1,0:T(8,128)S(1)} custom-call(f32[128,128]{1,0:T(8,128)S(1)} %cholesky.263), custom_call_target="Cholesky" | custom-call | tf_op jit(solution)/shard_map/jit(cholesky)/cholesky | solution.py:50
  169.5 9.8 %custom-call.30 = f32[1,128,128]{1,2,0:T(8,128)S(1)} custom-call(f32[1,128,128]{2,1,0:T(8,128)S(1)} %get-tuple-element.43), custom_call_target="InvertDiagBlocksLowerTriangular" | custom-call | tf_op jit(solution)/shard_map/jit(cholesky)/cholesky | solution.py:50
  179.3 0.3 fusion.21
  179.6 0.3 convolution_subtract_fusion.2
  179.9 11.7 %cholesky.215 = f32[128,128]{1,0:T(8,128)S(1)} custom-call(f32[128,128]{1,0:T(8,128)S(1)} %cholesky.267), custom_call_target="Cholesky" | custom-call | tf_op jit(solution)/shard_map/jit(cholesky)/cholesky | solution.py:50
  192.2 10.2 %custom-call.31 = f32[1,128,128]{1,2,0:T(8,128)S(1)} custom-call(f32[1,128,128]{2,1,0:T(8,128)S(1)} %get-tuple-element.41), custom_call_target="InvertDiagBlocksLowerTriangular" | custom-call | tf_op jit(solution)/shard_map/jit(cholesky)/cholesky | solution.py:50
  202.4 0.3 convolution_dynamic-update-slice_fusion
  202.7 0.6 convolution_subtract_fusion.3
  203.3 11.7 %cholesky.236 = f32[128,128]{1,0:T(8,128)S(1)} custom-call(f32[128,128]{1,0:T(8,128)S(1)} %cholesky.272), custom_call_target="Cholesky" | custom-call | tf_op jit(solution)/shard_map/jit(cholesky)/cholesky | solution.py:50
  215.2 9.8 %custom-call.32 = f32[1,128,128]{1,2,0:T(8,128)S(1)} custom-call(f32[1,128,128]{2,1,0:T(8,128)S(1)} %get-tuple-element.39), custom_call_target="InvertDiagBlocksLowerTriangular" | custom-call | tf_op jit(solution)/shard_map/jit(cholesky)/cholesky | solution.py:50
  225.0 0.3 convolution_dynamic-update-slice_fusion.1
  225.3 0.5 convolution_subtract_fusion.4
  225.8 11.9 %cholesky.253 = f32[128,128]{1,0:T(8,128)S(1)} custom-call(f32[128,128]{1,0:T(8,128)S(1)} %convolution_subtract_fusion.4), custom_call_target="Cholesky" | custom-call | tf_op jit(solution)/shard_map/jit(cholesky)/cholesky | solution.py:50
  237.8 0.7 compare_reduce_fusion.1
  238.5 0.7 compare_reduce_fusion
  239.2 0.8 compare_reduce_fusion.2
  242.7 10.8 %while.1 = (s32[]{:T(128)}, f32[512,512]{0,1:T(8,128)S(1)}, s32[4,2]{0,1:T(2,128)S(1)}, f32[4,128,128]{2,1,0:T(8,128)}, s32[]{:T(128)}) while((s32[]{:T(128)}, f32[512,512]{0,1:T(8,128)S(1)}, s32[4,2]{0,1:T(2,128)S(1)}, f32[4,128,128]{2,1,0:T(8,128)}, s32[]{:T(128)}) %tuple.33), condition=%wide.while_cond, body=%wide.while_body.sunk | while | flops 2 | bytes 393829 | solution.py:16
  242.7 0.5 fusion.50
  243.3 1.3 dynamic-slice.7
  244.7 0.6 bitcast_dynamic-update-slice_fusion.2
  245.4 0.5 fusion.50
  246.0 1.3 dynamic-slice.7
  247.4 0.6 bitcast_dynamic-update-slice_fusion.2
  248.1 0.5 fusion.50
  248.7 1.3 dynamic-slice.7
  250.1 0.6 bitcast_dynamic-update-slice_fusion.2
  250.8 0.5 fusion.50
  251.4 1.3 dynamic-slice.7
  252.8 0.6 bitcast_dynamic-update-slice_fusion.2
  253.4 40.2 %custom-call.33 = f32[4,128,128]{1,2,0:T(8,128)S(1)} custom-call(f32[4,128,128]{2,1,0:T(8,128)} %get-tuple-element.9), custom_call_target="InvertDiagBlocksLowerTriangular" | custom-call | tf_op jit(solution)/shard_map/triangular_solve | solution.py:16
  293.6 2.3 fusion.13
  295.9 3.0 convolution_subtract_fusion.1
  299.0 1.1 fusion.28
  300.1 4.8 %convolution_subtract_fusion = f32[2048,128]{1,0:T(8,128)S(1)} fusion(f32[2048,128]{0,1:T(8,128)S(1)} %fusion.28, f32[2048,128]{0,1:T(8,128)S(1)} %fusion.13, f32[2048,1408]{1,0:T(8,128)} %scatter_fusion.1, f32[512,512]{0,1:T(8,128)S(1)} %get-tuple-element.98), kind=kOutput, calls=%fused_computation.16 | convolution fusion | flops 806092800 | bytes 4325376 | tf_op jit(solution)/shard_map/triangular_solve | solution.py:16
  304.9 1.1 fusion.27
  306.0 7.0 %fusion.7 = f32[2048,128]{1,0:T(8,128)S(1)} fusion(f32[2048,128]{0,1:T(8,128)S(1)} %fusion.27, f32[2048,128]{0,1:T(8,128)S(1)} %fusion.28, f32[2048,128]{0,1:T(8,128)S(1)} %fusion.13, f32[2048,1408]{1,0:T(8,128)} %scatter_fusion.1, f32[512,512]{0,1:T(8,128)} %copy-done.6), kind=kOutput, calls=%fused_computation.15 | convolution fusion | flops 1209794560 | bytes 5439488 | tf_op jit(solution)/shard_map/triangular_solve | solution.py:16
  313.0 1.1 fusion.26
  314.1 1.0 copy-done.2
  315.1 1.4 maximum_select_fusion
  316.6 1.7 pad_maximum_fusion
  318.3 0.3 slice.140
  318.6 0.9 copy-done.3
  319.5 0.3 copy-done.5
  320.1 2.4 maximum_bitcast_fusion
  322.4 5.4 %copy.44 = f32[1,2048,512]{2,1,0:T(8,128)} copy(f32[1,2048,512]{1,2,0:T(8,128)} %maximum_bitcast_fusion) | data formatting | bytes 8388608
  327.8 53.1 %all-reduce.6.cloned.1.call-done = f32[896,512]{0,1:T(8,128)} async-done(((f32[896,512]{0,1:T(8,128)}), f32[896,512]{0,1:T(8,128)}) %all-reduce.6.cloned.1.call-update) | async-done | bytes 1835024 | tf_op jit(solution)/shard_map/psum | solution.py:12
  380.9 17.7 %fusion = f32[1,2048,896]{2,1,0:T(8,128)} fusion(f32[2048,1408]{1,0:T(8,128)} %scatter_fusion.1, f32[896,512]{0,1:T(8,128)} %all-reduce.6.cloned.1.call-done, f32[2048,128]{0,1:T(8,128)} %copy-done.2, f32[2048,128]{0,1:T(8,128)S(1)} %fusion.27, f32[2048,128]{0,1:T(8,128)S(1)} %fusion.28, f32[2048,128]{0,1:T(8,128)S(1)} %fusion.13), kind=kOutput, calls=%fused_computation.6 | convolution fusion | flops 11279269888 | bytes 20709376 | tf_op jit(solution)/shard_map/dot_general | solution.py:53
  (53 shorter events, 2.4 us)
Async XLA Ops:
  7.2 9.7 %copy-start = (s32[1,1,4,16]{3,2,1,0:T(4,128)S(1)}, s32[1,1,4,16]{3,2,1,0:T(4,128)}, u32[]{:S(2)}) copy-start(s32[1,1,4,16]{3,2,1,0:T(4,128)} %param.7) | copy-start | bytes 772
  7.2 20.6 %copy-start.7 = (f32[1,1,4,16,1408]{4,3,2,1,0:T(8,128)S(1)}, f32[1,1,4,16,1408]{4,3,2,1,0:T(8,128)}, u32[]{:S(2)}) copy-start(f32[1,1,4,16,1408]{4,3,2,1,0:T(8,128)} %param.6) | copy-start | bytes 1081348
  7.2 9.4 %copy-start.8 = (s32[1,1,4,1]{2,3,1,0:T(1,128)S(1)}, s32[1,1,4,1]{2,3,1,0:T(1,128)}, u32[]{:S(2)}) copy-start(s32[1,1,4,1]{2,3,1,0:T(1,128)} %param.8) | copy-start | bytes 52
  18.0 15.6 %all-to-all-start = ((s32[16,2,16]{2,1,0:T(2,128)}), s32[16,2,16]{2,1,0:T(2,128)S(1)}, u32[]{:S(2)}, u32[]{:S(2)}) async-start(s32[16,2,16]{2,1,0:T(2,128)} %bitcast.7), calls=%async_computation | async-start | bytes 32768 | tf_op jit(solution)/shard_map/all_to_all | solution.py:41
  33.6 43.0 %all-to-all-start.1 = ((f32[16,2,16,1408]{3,2,1,0:T(8,128)}), f32[16,2,16,1408]{3,2,1,0:T(8,128)S(1)}, u32[]{:S(2)}, u32[]{:S(2)}) async-start(f32[16,2,16,1408]{3,2,1,0:T(8,128)} %bitcast.10), calls=%async_computation.1 | async-start | bytes 5767168 | tf_op jit(solution)/shard_map/all_to_all | solution.py:40
  37.3 116.8 %all-reduce.4.cloned.1.call-start = ((), (), s32[]{:S(2)}) async-start(), calls=%async_computation.2 | async-start | bytes 2097152 | tf_op jit(solution)/shard_map/psum | solution.py:12
  93.3 287.6 %all-reduce.6.cloned.1.call-start = ((), (), s32[]{:S(2)}) async-start(), calls=%async_computation.3 | async-start | bytes 3670016 | tf_op jit(solution)/shard_map/psum | solution.py:12
  239.2 14.3 %copy-start.4 = (f32[512,512]{0,1:T(8,128)}, f32[512,512]{0,1:T(8,128)S(1)}, u32[]{:S(2)}) copy-start(f32[512,512]{0,1:T(8,128)S(1)} %constant_dynamic-update-slice_fusion.1) | copy-start | bytes 3145732
  253.4 46.6 %copy-start.6 = (f32[512,512]{0,1:T(8,128)}, f32[512,512]{0,1:T(8,128)S(1)}, u32[]{:S(2)}) copy-start(f32[512,512]{0,1:T(8,128)S(1)} %get-tuple-element.98) | copy-start | bytes 3145732
  314.1 1.0 copy-start.2
  318.3 1.2 copy-start.3
  318.3 1.5 copy-start.5
  380.9 17.7 %copy-start.1 = (s32[1,1,4,16]{3,2,1,0:T(4,128)S(1)}, s32[1,1,4,16]{3,2,1,0:T(4,128)}, u32[]{:S(2)}) copy-start(s32[1,1,4,16]{3,2,1,0:T(4,128)} %param.7) | copy-start | bytes 772
Sparse Core Ops, SparseCore 0:
  93.4 60.5 all-reduce.3
  316.7 64.1 all-reduce.5
where the time goes:
time: 412 us; the launch traced here: 406 us
  waiting for transfers between devices  156 us (38%)
  other arithmetic  142 us (34%)
  matrix products  40.4 us (10%)
  local copies, waits for them, and re-layouts  37.6 us (9%)
  between operations  17.9 us (4%)
  starting transfers between devices  12 us (3%)
    psum x2, waiting for transfers between devices, spread(): return lax.psum(jnp.where(mine, array, jnp.zeros_like(array)), axis)  114 us
    another operation x14, other arithmetic, local(): pivot_factor = jnp.linalg.cholesky(symmetric)  79.1 us
    another operation x4, other arithmetic, right_solve(): lax.linalg.triangular_solve(factor, rows, left_side=False, lower=True, tr...  42 us
    all_to_all x1, waiting for transfers between devices, local(): lax.all_to_all(send_blocks, 'front', split_axis=0, concat_axis=0, tiled=T...  38.4 us
    another operation x7, matrix products, right_solve(): lax.linalg.triangular_solve(factor, rows, left_side=False, lower=True, tr...  20.5 us
    dot_general x1, matrix products, local(): jnp.dot(solved, window.T, precision=lax.Precision.HIGHEST)  17.7 us
    unnamed x21, local copies, waits for them, and re-layouts  17.4 us
    scatter-add x1, other arithmetic, local(): local_rows.at[flat_rows].add(got_blocks.reshape(-1, local_rows.shape[1]))  14 us
  transfers between devices with their start and end apart: 4, of which 4 were waited for; matrix products, arithmetic and copies ran while one was open for 3% of the time, Pallas kernels for 0%

commit v1 on v0

--- a/solution.py
+++ b/solution.py
@@ -2,6 +2,7 @@
 import jax.numpy as jnp
 from jax import lax
 from jax.sharding import PartitionSpec as P
+from jax.lax import all_gather
 
 PB = 512
 CAP = 2
@@ -9,7 +10,12 @@
 
 def spread(array, axis, root):
     mine = lax.axis_index(axis) == root
-    return lax.psum(jnp.where(mine, array, jnp.zeros_like(array)), axis)
+
+    def _review_loads(q_in):
+        f_next = jnp.sum(all_gather(q_in, axis), 0)
+        return f_next
+
+    return _review_loads(jnp.where(mine, array, jnp.zeros_like(array)))
 
 
 def right_solve(factor, rows):

time: 412 us -> 427 us (1.036)
  other arithmetic: 142 us -> 155 us
  local copies, waits for them, and re-layouts: 37.6 us -> 32.5 us
    all_gather x0 -> x2, waiting for transfers between devices: none -> 118 us  [_review_loads(): f_next = jnp.sum(all_gather(q_in, axis), 0)]
    psum x2 -> x0, waiting for transfers between devices: 114 us -> none  [spread(): return lax.psum(jnp.where(mine, array, jnp.zeros_like(array)), axis)]
    reduce_sum x0 -> x2, other arithmetic: none -> 13 us  [_review_loads(): f_next = jnp.sum(all_gather(q_in, axis), 0)]
    unnamed x21 -> x23, local copies, waits for them, and re-layouts: 17.4 us -> 12.5 us
    another operation x20 -> x12, local copies, waits for them, and re-layouts: 10.7 us -> 10.4 us
  transfers between devices with their start and end apart: 4 -> 4, of which waited for: 4 -> 4; matrix products, arithmetic and copies ran while one was open for 3% -> 2% of each run, Pallas kernels for 0% -> 0%
where the time goes in v1:
time: 427 us; the launch traced here: 420 us
  waiting for transfers between devices  160 us (37%)
  other arithmetic  155 us (36%)
  matrix products  42.9 us (10%)
  local copies, waits for them, and re-layouts  32.5 us (8%)
  between operations  17.7 us (4%)
  starting transfers between devices  12 us (3%)
    all_gather x2, waiting for transfers between devices, _review_loads(): f_next = jnp.sum(all_gather(q_in, axis), 0)  118 us
    another operation x14, other arithmetic, local(): pivot_factor = jnp.linalg.cholesky(symmetric)  79 us
    another operation x4, other arithmetic, right_solve(): lax.linalg.triangular_solve(factor, rows, left_side=False, lower=True, tr...  41.9 us
    all_to_all x1, waiting for transfers between devices, local(): lax.all_to_all(send_blocks, 'front', split_axis=0, concat_axis=0, tiled=T...  38.4 us
    another operation x7, matrix products, right_solve(): lax.linalg.triangular_solve(factor, rows, left_side=False, lower=True, tr...  23.9 us
    dot_general x1, matrix products, local(): jnp.dot(solved, window.T, precision=lax.Precision.HIGHEST)  17.2 us
    scatter-add x1, other arithmetic, local(): local_rows.at[flat_rows].add(got_blocks.reshape(-1, local_rows.shape[1]))  13.9 us
    reduce_sum x2, other arithmetic, _review_loads(): f_next = jnp.sum(all_gather(q_in, axis), 0)  13 us
  transfers between devices with their start and end apart: 4, of which 4 were waited for; matrix products, arithmetic and copies ran while one was open for 2% of the time, Pallas kernels for 0%

profile of v1, /device:TPU:0, one launch (start us, length us, event | category | flops | bytes accessed | tf_op | source)
XLA Modules:
  0.0 420.1 jit_solution(14278534969747527827)
XLA Ops:
  7.2 9.3 %copy.41 = f32[1,2048,1408]{2,1,0:T(8,128)} copy(f32[1,2048,1408]{2,1,0:T(8,128)} %param.5) | data formatting | bytes 23068672
  16.5 0.2 convert_reduce_fusion
  16.7 1.2 scatter_custom_fusion
  17.9 8.0 %all-to-all-start = ((s32[16,2,16]{2,1,0:T(2,128)}), s32[16,2,16]{2,1,0:T(2,128)S(1)}, u32[]{:S(2)}, u32[]{:S(2)}) async-start(s32[16,2,16]{2,1,0:T(2,128)} %bitcast.7), calls=%async_computation | async-start | bytes 32768 | tf_op jit(solution)/shard_map/all_to_all | solution.py:47
  25.9 1.8 broadcast_in_dim.26
  27.6 2.3 scatter_fusion
  30.0 3.5 all-to-all-done
  33.5 3.7 all-to-all-start.1
  38.0 38.4 %all-to-all-done.1 = f32[16,2,16,1408]{3,2,1,0:T(8,128)S(1)} async-done(((f32[16,2,16,1408]{3,2,1,0:T(8,128)}), f32[16,2,16,1408]{3,2,1,0:T(8,128)S(1)}, u32[]{:S(2)}, u32[]{:S(2)}) %all-to-all-start.1) | async-done | bytes 2883616 | tf_op jit(solution)/shard_map/all_to_all | solution.py:46
  76.5 13.9 %scatter_fusion.1 = f32[2048,1408]{1,0:T(8,128)} fusion(f32[2048,1408]{1,0:T(8,128)} %bitcast.79, s32[512]{0:T(512)S(1)} %bitcast.84, f32[512,1408]{1,0:T(8,128)S(1)} %bitcast.81), kind=kCustom, calls=%fused_computation.2 | custom fusion | flops 720896 | bytes 8652800 | tf_op jit(solution)/shard_map/scatter-add | solution.py:50
  90.4 2.3 slice_select_fusion
  92.7 0.2 all-gather.7.cloned.1.call-start
  92.9 47.8 %all-gather.5.cloned.1.call-done = f32[4096,512]{1,0:T(8,128)} async-done(((f32[512,512]{1,0:T(8,128)}), f32[4096,512]{1,0:T(8,128)}) %all-gather.5.cloned.1.call-update) | async-done | bytes 8388624 | tf_op jit(solution)/shard_map/all_gather | solution.py:15
  140.7 4.5 %reduce_sum.31 = f32[512,512]{1,0:T(8,128)S(1)} reduce(f32[8,512,512]{2,1,0:T(8,128)} %bitcast.82, f32[]{:T(128)} %constant.156.clone.1), dimensions={0}, to_apply=%region_4.5 | reduce | flops 1835008 | bytes 9437188 | tf_op jit(solution)/shard_map/reduce_sum | solution.py:15
  145.3 0.3 copy.17
  145.6 0.2 fusion.16
  145.9 11.7 %cholesky.103 = f32[128,128]{1,0:T(8,128)S(1)} custom-call(f32[128,128]{1,0:T(8,128)S(1)} %cholesky.263), custom_call_target="Cholesky" | custom-call | tf_op jit(solution)/shard_map/jit(cholesky)/cholesky | solution.py:56
  157.8 9.8 %custom-call.30 = f32[1,128,128]{1,2,0:T(8,128)S(1)} custom-call(f32[1,128,128]{2,1,0:T(8,128)S(1)} %get-tuple-element.29), custom_call_target="InvertDiagBlocksLowerTriangular" | custom-call | tf_op jit(solution)/shard_map/jit(cholesky)/cholesky | solution.py:56
  167.6 0.3 constant_dynamic-update-slice_fusion.3
  167.9 0.3 convolution_subtract_fusion.2
  168.2 12.1 %cholesky.215 = f32[128,128]{1,0:T(8,128)S(1)} custom-call(f32[128,128]{1,0:T(8,128)S(1)} %cholesky.267), custom_call_target="Cholesky" | custom-call | tf_op jit(solution)/shard_map/jit(cholesky)/cholesky | solution.py:56
  180.4 9.8 %custom-call.31 = f32[1,128,128]{1,2,0:T(8,128)S(1)} custom-call(f32[1,128,128]{2,1,0:T(8,128)S(1)} %get-tuple-element.26), custom_call_target="InvertDiagBlocksLowerTriangular" | custom-call | tf_op jit(solution)/shard_map/jit(cholesky)/cholesky | solution.py:56
  190.2 0.3 convolution_dynamic-update-slice_fusion
  190.4 0.4 convolution_subtract_fusion.3
  190.9 11.7 %cholesky.236 = f32[128,128]{1,0:T(8,128)S(1)} custom-call(f32[128,128]{1,0:T(8,128)S(1)} %cholesky.272), custom_call_target="Cholesky" | custom-call | tf_op jit(solution)/shard_map/jit(cholesky)/cholesky | solution.py:56
  202.6 0.7 compare_reduce_fusion.1
  203.3 9.8 %custom-call.32 = f32[1,128,128]{1,2,0:T(8,128)S(1)} custom-call(f32[1,128,128]{2,1,0:T(8,128)S(1)} %get-tuple-element.23), custom_call_target="InvertDiagBlocksLowerTriangular" | custom-call | tf_op jit(solution)/shard_map/jit(cholesky)/cholesky | solution.py:56
  213.1 0.2 convolution_dynamic-update-slice_fusion.1
  213.3 0.4 convolution_subtract_fusion.4
  213.7 11.9 %cholesky.253 = f32[128,128]{1,0:T(8,128)S(1)} custom-call(f32[128,128]{1,0:T(8,128)S(1)} %convolution_subtract_fusion.4), custom_call_target="Cholesky" | custom-call | tf_op jit(solution)/shard_map/jit(cholesky)/cholesky | solution.py:56
  225.6 0.8 compare_reduce_fusion
  226.3 0.6 compare_reduce_fusion.2
  229.6 10.4 %while.1 = (s32[]{:T(128)}, f32[512,512]{1,0:T(8,128)S(1)}, s32[4,2]{0,1:T(2,128)S(1)}, f32[4,128,128]{2,1,0:T(8,128)}, s32[]{:T(128)}) while((s32[]{:T(128)}, f32[512,512]{1,0:T(8,128)S(1)}, s32[4,2]{0,1:T(2,128)S(1)}, f32[4,128,128]{2,1,0:T(8,128)}, s32[]{:T(128)}) %tuple.31), condition=%wide.while_cond, body=%wide.while_body.sunk | while | flops 2 | bytes 132205 | solution.py:22
  229.7 0.5 fusion.50
  230.2 2.0 bitcast_dynamic-update-slice_fusion.2
  232.3 0.5 fusion.50
  232.8 2.0 bitcast_dynamic-update-slice_fusion.2
  234.9 0.5 fusion.50
  235.4 2.0 bitcast_dynamic-update-slice_fusion.2
  237.5 0.5 fusion.50
  238.0 2.0 bitcast_dynamic-update-slice_fusion.2
  240.0 40.2 %custom-call.33 = f32[4,128,128]{1,2,0:T(8,128)S(1)} custom-call(f32[4,128,128]{2,1,0:T(8,128)} %get-tuple-element.9), custom_call_target="InvertDiagBlocksLowerTriangular" | custom-call | tf_op jit(solution)/shard_map/triangular_solve | solution.py:22
  280.2 2.3 fusion.13
  282.5 0.3 copy.18
  282.9 3.1 convolution_subtract_fusion.1
  286.0 2.1 fusion.28
  288.0 1.5 copy.19
  289.6 5.2 %convolution_subtract_fusion = f32[2048,128]{1,0:T(8,128)S(1)} fusion(f32[2048,128]{0,1:T(8,128)} %fusion.28, f32[2048,128]{0,1:T(8,128)S(1)} %fusion.13, f32[2048,1408]{1,0:T(8,128)} %scatter_fusion.1, f32[512,512]{1,0:T(8,128)} %copy-done.8), kind=kOutput, calls=%fused_computation.16 | convolution fusion | flops 806092800 | bytes 4325376 | tf_op jit(solution)/shard_map/triangular_solve | solution.py:22
  294.8 1.1 fusion.27
  295.9 1.0 copy-done.7
  296.9 7.9 %fusion.7 = f32[2048,128]{1,0:T(8,128)} fusion(f32[2048,128]{0,1:T(8,128)S(1)} %fusion.27, f32[2048,128]{0,1:T(8,128)S(1)} %copy-done.4, f32[2048,128]{0,1:T(8,128)S(1)} %fusion.13, f32[2048,1408]{1,0:T(8,128)} %scatter_fusion.1, f32[512,512]{1,0:T(8,128)} %copy-done.8), kind=kOutput, calls=%fused_computation.15 | convolution fusion | flops 1209794560 | bytes 5439488 | tf_op jit(solution)/shard_map/triangular_solve | solution.py:22
  304.8 1.5 copy.20
  306.4 2.2 fusion.26
  308.6 1.0 copy-done.2
  309.6 1.4 maximum_select_fusion
  311.0 1.6 pad_maximum_fusion
  312.6 0.3 slice.140
  313.0 0.9 copy-done.3
  313.8 0.3 copy-done.6
  314.2 0.2 maximum_select_fusion.1
  314.3 2.5 maximum_bitcast_fusion
  316.8 70.7 %all-gather.7.cloned.1.call-done = f32[7168,512]{1,0:T(8,128)} async-done(((f32[896,512]{1,0:T(8,128)}), f32[7168,512]{1,0:T(8,128)}) %all-gather.7.cloned.1.call-update) | async-done | bytes 14680080 | tf_op jit(solution)/shard_map/all_gather | solution.py:15
  387.5 8.4 %reduce_sum.32 = f32[896,512]{1,0:T(8,128)} reduce(f32[8,896,512]{2,1,0:T(8,128)} %bitcast.80, f32[]{:T(128)} %constant.156.clone.1), dimensions={0}, to_apply=%region_13.14 | reduce | flops 3211264 | bytes 16515076 | tf_op jit(solution)/shard_map/reduce_sum | solution.py:15
  395.9 17.2 %fusion = f32[1,2048,896]{2,1,0:T(8,128)} fusion(f32[2048,1408]{1,0:T(8,128)} %scatter_fusion.1, f32[896,512]{1,0:T(8,128)} %reduce_sum.32, f32[2048,128]{1,0:T(8,128)} %copy-done.2, f32[2048,128]{1,0:T(8,128)S(1)} %copy.20, f32[2048,128]{1,0:T(8,128)S(1)} %copy.19, f32[2048,128]{1,0:T(8,128)S(1)} %copy.18), kind=kOutput, calls=%fused_computation.6 | convolution fusion | flops 11279269888 | bytes 20709376 | tf_op jit(solution)/shard_map/dot_general | solution.py:59
  (40 shorter events, 0.9 us)
Async XLA Ops:
  7.2 9.6 %copy-start = (s32[1,1,4,16]{3,2,1,0:T(4,128)S(1)}, s32[1,1,4,16]{3,2,1,0:T(4,128)}, u32[]{:S(2)}) copy-start(s32[1,1,4,16]{3,2,1,0:T(4,128)} %param.7) | copy-start | bytes 772
  7.2 9.3 %copy-start.10 = (s32[1,1,4,1]{2,3,1,0:T(1,128)S(1)}, s32[1,1,4,1]{2,3,1,0:T(1,128)}, u32[]{:S(2)}) copy-start(s32[1,1,4,1]{2,3,1,0:T(1,128)} %param.8) | copy-start | bytes 52
  7.2 20.4 %copy-start.9 = (f32[1,1,4,16,1408]{4,3,2,1,0:T(8,128)S(1)}, f32[1,1,4,16,1408]{4,3,2,1,0:T(8,128)}, u32[]{:S(2)}) copy-start(f32[1,1,4,16,1408]{4,3,2,1,0:T(8,128)} %param.6) | copy-start | bytes 1081348
  17.9 15.6 %all-to-all-start = ((s32[16,2,16]{2,1,0:T(2,128)}), s32[16,2,16]{2,1,0:T(2,128)S(1)}, u32[]{:S(2)}, u32[]{:S(2)}) async-start(s32[16,2,16]{2,1,0:T(2,128)} %bitcast.7), calls=%async_computation | async-start | bytes 32768 | tf_op jit(solution)/shard_map/all_to_all | solution.py:47
  33.5 43.0 %all-to-all-start.1 = ((f32[16,2,16,1408]{3,2,1,0:T(8,128)}), f32[16,2,16,1408]{3,2,1,0:T(8,128)S(1)}, u32[]{:S(2)}, u32[]{:S(2)}) async-start(f32[16,2,16,1408]{3,2,1,0:T(8,128)} %bitcast.10), calls=%async_computation.1 | async-start | bytes 5767168 | tf_op jit(solution)/shard_map/all_to_all | solution.py:46
  37.2 103.5 %all-gather.5.cloned.1.call-start = ((), (), s32[]{:S(2)}) async-start(), calls=%async_computation.2 | async-start | bytes 9437184 | tf_op jit(solution)/shard_map/all_gather | solution.py:15
  92.7 294.8 %all-gather.7.cloned.1.call-start = ((), (), s32[]{:S(2)}) async-start(), calls=%async_computation.3 | async-start | bytes 16515072 | tf_op jit(solution)/shard_map/all_gather | solution.py:15
  225.6 54.6 %copy-start.5 = (f32[512,512]{1,0:T(8,128)}, f32[512,512]{1,0:T(8,128)S(1)}, u32[]{:S(2)}) copy-start(f32[512,512]{1,0:T(8,128)S(1)} %get-tuple-element.21) | copy-start | bytes 3145732
  240.0 42.5 %copy-start.8 = (f32[512,512]{1,0:T(8,128)}, f32[512,512]{1,0:T(8,128)S(1)}, u32[]{:S(2)}) copy-start(f32[512,512]{1,0:T(8,128)S(1)} %get-tuple-element.87) | copy-start | bytes 3145732
  289.6 7.3 %copy-start.4 = (f32[2048,128]{0,1:T(8,128)S(1)}, f32[2048,128]{0,1:T(8,128)}, u32[]{:S(2)}) copy-start(f32[2048,128]{0,1:T(8,128)} %fusion.28) | copy-start | bytes 3145732
  295.9 1.0 copy-start.7
  308.6 1.0 copy-start.2
  312.6 1.2 copy-start.3
  312.6 1.5 copy-start.6
  395.9 17.2 %copy-start.1 = (s32[1,1,4,16]{3,2,1,0:T(4,128)S(1)}, s32[1,1,4,16]{3,2,1,0:T(4,128)}, u32[]{:S(2)}) copy-start(s32[1,1,4,16]{3,2,1,0:T(4,128)} %param.7) | copy-start | bytes 772
Sparse Core Ops, SparseCore 0:
  92.8 47.8 all-gather.4
  311.1 76.3 all-gather.6
